TPU v7x, 32 devices: a whole 2x2x4 slice. The times are simulated.
32 devices in a mesh: fsdp: 8 (over z, y), tp: 4 (over x, core).
Axes of the slice: x: 2, y: 2, z: 4, core: 2. Of those that a mesh axis runs over, the one named last changes fastest.
Arguments:
- dout: bfloat16 [2048, 4096], P('fsdp', 'tp'), may hold values from -6 to 6
- w_out: bfloat16 [8192, 4096], P(('tp', 'fsdp')), may hold values from -0.09375 to 0.09375
- y_scan: bfloat16 [2048, 8192], P('fsdp', 'tp'), may hold values from -6 to 6
- z_gate: bfloat16 [2048, 8192], P('fsdp', 'tp'), may hold values from -6 to 6
- x_conv: bfloat16 [2048, 8192], P('fsdp', 'tp'), may hold values from -6 to 6
- du_scan: bfloat16 [2048, 8192], P('fsdp', 'tp'), may hold values from -9 to 9
- conv_w: float32 [4, 8192], P(None, 'tp'), may hold values from -3 to 3
- conv_b: float32 [8192], P('tp'), may hold values from -1 to 1
Outputs:
- d_y: bfloat16 [2048, 8192], P('fsdp', 'tp')
- d_z: bfloat16 [2048, 8192], P('fsdp', 'tp')
- d_x: bfloat16 [2048, 8192], P('fsdp', 'tp')
- d_conv_w: float32 [4, 8192], P(None, 'tp')
- d_conv_b: float32 [8192], P('tp')
All inputs are finite; a program needn't handle non-finite values.
Results may differ from a plain program's by a relative error of at most 0.001.
Values may be sent and summed in bfloat16 or wider, within the bound.
A program may use at most 64 MiB of HBM per device.

v0:
```python
import jax
import jax.numpy as jnp
from jax import lax
from jax.sharding import PartitionSpec as P

KW = 4


def shifted(block, axis, distance):
    devices = range(lax.axis_size(axis))
    route = [(i - distance, i) for i in devices if i - distance in devices]
    return lax.ppermute(block, axis, route)


def silu_slope(value):
    sig = jax.nn.sigmoid(value)
    return sig * (1.0 + value * (1.0 - sig))


def local(dout, w_out, y_scan, z_gate, x_conv, du_scan, conv_w, conv_b):
    tok_rows = x_conv.shape[0]
    width = x_conv.shape[1]
    prior = shifted(x_conv[tok_rows - (KW - 1) :], "fsdp", 1)
    leading = jnp.stack([x_conv[: KW - 1], du_scan[: KW - 1]])
    later = shifted(leading, "fsdp", -1)
    extended = jnp.concatenate([prior, x_conv, later[0]], 0)
    span = tok_rows + KW - 1
    pre_all = jnp.zeros((span, width), jnp.float32) + conv_b[None, :]
    for k in range(KW):
        pre_all = pre_all + conv_w[k][None, :] * extended[k : k + span]
    arriving = jnp.concatenate([du_scan, later[1]], 0)
    d_pre_all = arriving.astype(jnp.float32) * silu_slope(pre_all)
    d_pre = d_pre_all[:tok_rows]
    grad_x = jnp.zeros((tok_rows, width), jnp.float32)
    taps = []
    for k in range(KW):
        grad_x = grad_x + conv_w[k][None, :] * d_pre_all[KW - 1 - k : KW - 1 - k + tok_rows]
        taps.append(jnp.sum(d_pre * extended[k : k + tok_rows], 0))
    grad_w, grad_b = lax.psum((jnp.stack(taps), jnp.sum(d_pre, 0)), "fsdp")
    full_out = lax.all_gather(dout, "tp", axis=1, tiled=True)
    group_w = lax.all_gather(w_out, "fsdp", axis=0, tiled=True)
    d_gated = lax.dot_general(
        full_out, group_w, (((1,), (1,)), ((), ())), preferred_element_type=jnp.float32
    )
    gate_f = z_gate.astype(jnp.float32)
    grad_y = (d_gated * jax.nn.silu(gate_f)).astype(jnp.bfloat16)
    grad_z = (d_gated * y_scan.astype(jnp.float32) * silu_slope(gate_f)).astype(jnp.bfloat16)
    return (grad_y, grad_z, grad_x.astype(jnp.bfloat16), grad_w, grad_b)


def solution(mesh):
    return jax.shard_map(
        local,
        mesh=mesh,
        in_specs=(
            P("fsdp", "tp"),
            P(("tp", "fsdp"), None),
            P("fsdp", "tp"),
            P("fsdp", "tp"),
            P("fsdp", "tp"),
            P("fsdp", "tp"),
            P(None, "tp"),
            P("tp"),
        ),
        out_specs=(P("fsdp", "tp"), P("fsdp", "tp"), P("fsdp", "tp"), P(None, "tp"), P("tp")),
        check_vma=False,
    )
```

profile of v0, /device:TPU:0, one launch (start us, length us, event | category | flops | bytes accessed | tf_op | source)
XLA Modules:
  0.0 284.7 jit_solution(4298243487837612231)
XLA Ops:
  7.2 0.0 copy-start
  7.2 0.0 copy-start.1
  7.2 0.0 copy-start.2
  7.2 0.0 all-gather.3.cloned.1.call-start
  7.2 0.7 all-gather.3.cloned.1.call-update
  7.9 0.0 copy-start.3
  7.9 0.0 all-gather.5.cloned.1.call-start
  8.0 0.7 all-gather.5.cloned.1.call-update
  8.7 0.0 copy-done
  8.7 4.9 %collective-permute-start.1 = (bf16[3,2048]{1,0:T(4,128)(2,1)S(1)}, bf16[3,2048]{1,0:T(4,128)(2,1)S(1)}, u32[]{:S(2)}, u32[]{:S(2)}) collective-permute-start(bf16[3,2048]{1,0:T(4,128)(2,1)S(1)} %get-tuple-element.16), channel_id=1, source_target_pairs={{0,4},{4,8},{8,12},{12,16},{16,20},{20,24},{24,28},{1,5},{5,9},{9,... | collective-permute-start | bytes 36872 | tf_op jit(solution)/shard_map/ppermute | solution.py:12
  13.6 0.0 copy-done.1
  13.7 1.3 collective-permute-start
  15.0 0.0 copy-done.2
  15.0 4.5 %collective-permute-done = bf16[2,3,2048]{2,1,0:T(4,128)(2,1)S(1)} collective-permute-done((bf16[2,3,2048]{2,1,0:T(4,128)(2,1)S(1)}, bf16[2,3,2048]{2,1,0:T(4,128)(2,1)S(1)}, u32[]{:S(2)}, u32[]{:S(2)}) %collective-permute-start) | collective-permute-done | bytes 24608 | tf_op jit(solution)/shard_map/ppermute | solution.py:12
  19.5 0.0 collective-permute-done.1
  19.5 0.3 pad_maximum_fusion.1
  19.8 0.0 copy-done.3
  19.8 2.0 multiply_multiply_fusion
  21.8 0.0 copy-start.4
  21.8 0.0 copy-start.5
  21.9 3.0 %multiply_reduce_fusion.3 = (f32[2048]{0:T(1024)S(1)}, f32[2048]{0:T(1024)S(1)}, f32[2048]{0:T(1024)S(1)}, f32[2048]{0:T(1024)S(1)}, f32[2048]{0:T(1024)S(1)}, /*index=5*/bf16[256,2048]{1,0:T(8,128)(2,1)}) fusion(f32[259,2048]{1,0:T(8,128)S(1)} %multiply_multiply_fusion, bf16[3,2048]{1,0:T(4,128)(2,1)S(1)} %collective-permute-done.1, ...), kind=kLoop, calls=%fused_computation.27 | loop fusion | flops 15718400 | bytes 10571776 | tf_op jit(solution)/shard_map/reduce_sum | solution.py:38
  24.9 37.2 %all-reduce = (f32[4,2048]{1,0:T(4,128)}, f32[2048]{0:T(1024)}) all-reduce(f32[4,2048]{1,0:T(4,128)S(1)} %pad_maximum_fusion.3, f32[2048]{0:T(1024)S(1)} %get-tuple-element.9), channel_id=1, replica_groups=mesh['fsdp'=8,'tp'=4] {'fsdp'}, use_global_device_ids=true, to_apply=%region_4.0 | all-reduce | flops 10240 | bytes 81920 | tf_op jit(solution)/shard_map/psum | solution.py:39
  62.1 0.0 all-gather.3.cloned.1.call-done
  62.1 202.8 %all-gather.5.cloned.1.call-done = bf16[2048,4096]{1,0:T(8,128)(2,1)} async-done(((bf16[256,4096]{1,0:T(8,128)(2,1)}), bf16[2048,4096]{1,0:T(8,128)(2,1)}) %all-gather.5.cloned.1.call-update) | async-done | bytes 16777232 | tf_op jit(solution)/shard_map/all_gather | solution.py:41
  265.0 0.0 copy-done.4
  265.0 0.0 copy-done.5
  265.0 12.9 %fusion.8 = (bf16[256,2048]{1,0:T(8,128)(2,1)}, bf16[256,2048]{1,0:T(8,128)(2,1)}) fusion(bf16[256,2048]{1,0:T(8,128)(2,1)S(1)} %copy-done.4, bf16[256,2048]{1,0:T(8,128)(2,1)S(1)} %copy-done.5, bf16[256,4096]{1,0:T(8,128)(2,1)} %all-gather.3.cloned.1.call-done, bf16[2048,4096]{1,0:T(8,128)(2,1)} %all-gather.5.cloned.1.call-done), kind=kOutput, calls=%fused_computation.16 | convolution fusion | flops 4302831616 | bytes 23068672 | tf_op jit(solution)/shard_map/dot_general | solution.py:42
  (6 shorter events, 0.1 us)
Async XLA Ops:
  7.2 1.5 copy-start
  7.2 6.4 %copy-start.1 = (bf16[256,2048]{1,0:T(8,128)(2,1)S(1)}, bf16[256,2048]{1,0:T(8,128)(2,1)}, u32[]{:S(2)}) copy-start(bf16[256,2048]{1,0:T(8,128)(2,1)} %param.13) | copy-start | bytes 3145732
  7.2 7.8 %copy-start.2 = (f32[4,2048]{1,0:T(4,128)S(1)}, f32[4,2048]{1,0:T(4,128)}, u32[]{:S(2)}) copy-start(f32[4,2048]{1,0:T(4,128)} %param.14) | copy-start | bytes 98308
  7.2 54.9 %all-gather.3.cloned.1.call-start = ((), (), s32[]{:S(2)}) async-start(), calls=%async_computation | async-start | bytes 2621440 | tf_op jit(solution)/shard_map/all_gather | solution.py:40
  7.9 11.9 %copy-start.3 = (f32[2048]{0:T(1024)S(1)}, f32[2048]{0:T(1024)}, u32[]{:S(2)}) copy-start(f32[2048]{0:T(1024)} %param.15) | copy-start | bytes 24580
  7.9 257.0 %all-gather.5.cloned.1.call-start = ((), (), s32[]{:S(2)}) async-start(), calls=%async_computation.1 | async-start | bytes 18874368 | tf_op jit(solution)/shard_map/all_gather | solution.py:41
  8.7 10.8 %collective-permute-start.1 = (bf16[3,2048]{1,0:T(4,128)(2,1)S(1)}, bf16[3,2048]{1,0:T(4,128)(2,1)S(1)}, u32[]{:S(2)}, u32[]{:S(2)}) collective-permute-start(bf16[3,2048]{1,0:T(4,128)(2,1)S(1)} %get-tuple-element.16), channel_id=1, source_target_pairs={{0,4},{4,8},{8,12},{12,16},{16,20},{20,24},{24,28},{1,5},{5,9},{9,... | collective-permute-start | bytes 36872 | tf_op jit(solution)/shard_map/ppermute | solution.py:12
  13.7 5.8 %collective-permute-start = (bf16[2,3,2048]{2,1,0:T(4,128)(2,1)S(1)}, bf16[2,3,2048]{2,1,0:T(4,128)(2,1)S(1)}, u32[]{:S(2)}, u32[]{:S(2)}) collective-permute-start(bf16[2,3,2048]{2,1,0:T(4,128)(2,1)S(1)} %pad_maximum_fusion.2), channel_id=1, source_target_pairs={{4,0},{8,4},{12,8},{16,12},{20,16},{24,20},{28,24},{5,1},{9,5},{13... | collective-permute-start | bytes 73736 | tf_op jit(solution)/shard_map/ppermute | solution.py:12
  21.8 243.1 %copy-start.4 = (bf16[256,2048]{1,0:T(8,128)(2,1)S(1)}, bf16[256,2048]{1,0:T(8,128)(2,1)}, u32[]{:S(2)}) copy-start(bf16[256,2048]{1,0:T(8,128)(2,1)} %param.11) | copy-start | bytes 3145732
  21.8 243.1 %copy-start.5 = (bf16[256,2048]{1,0:T(8,128)(2,1)S(1)}, bf16[256,2048]{1,0:T(8,128)(2,1)}, u32[]{:S(2)}) copy-start(bf16[256,2048]{1,0:T(8,128)(2,1)} %param.10) | copy-start | bytes 3145732
Sparse Core Ops, SparseCore 0:
  9.6 25.2 all-gather.2
  37.0 227.8 all-gather.4
where the time goes:
time: 285 us
  waiting for transfers between devices  209 us (73%)
  blocking collectives  37.2 us (13%)
  between operations  14.2 us (5%)
  matrix products  12.9 us (5%)
  starting transfers between devices  6.24 us (2%)
  other arithmetic  5.35 us (2%)
    all_gather x1, waiting for transfers between devices, local(): group_w = lax.all_gather(w_out, 'fsdp', axis=0, tiled=True)  203 us
    psum x1, blocking collectives, local(): grad_w, grad_b = lax.psum((jnp.stack(taps), jnp.sum(d_pre, 0)), 'fsdp')  37.2 us
    dot_general x1, matrix products, local(): lax.dot_general(full_out, group_w, (((1,), (1,)), ((), ())), preferred_el...  12.9 us
    ppermute x2, starting transfers between devices, shifted(): return lax.ppermute(block, axis, route)  6.16 us
  transfers between devices with their start and end apart: 4, of which 2 were waited for; matrix products, arithmetic and copies ran while one was open for 2% of the time, Pallas kernels for 0%

commit v1 on v0

v1 whole, which is shorter than its diff:
```python
import functools

import jax
import jax.numpy as jnp
from jax import lax
from jax.experimental import pallas as pl
from jax.experimental.pallas import tpu as pltpu
from jax.sharding import PartitionSpec as P

KW = 4
HALO = 16
MESH = pl.DeviceIdType.MESH
F32 = jnp.float32
BF16 = jnp.bfloat16


def silu_slope(value):
    sig = jax.nn.sigmoid(value)
    return sig * (1.0 + value * (1.0 - sig))


def kernel(
    nf, nt, dout, w, y_in, z_in, x_in, du_in, cw, cb,
    oy, oz, ox, owb,
    dbuf, wo, wn, sbuf, rbuf, xb, ub, yb, zb, hp, hl, xe, ue, pe, tb, tr, tg,
    lsem, dr, zs, xs, cs, ws, wr, ss, rr, hs, hr, ts, trs, gs, gr,
):
    nz = nf // 2
    f = lax.axis_index("fsdp")
    t = lax.axis_index("tp")
    z, y = lax.div(f, 2), lax.rem(f, 2)
    x, c = lax.div(t, 2), lax.rem(t, 2)
    yf = z * 2 + 1 - y
    tx = (1 - x) * 2 + c
    tc = x * 2 + 1 - c
    tok, depth = dout.shape
    rows = w.shape[0]
    half = rows // 2

    def remote(src, dst, send, recv, fi, ti):
        return pltpu.make_async_remote_copy(
            src_ref=src, dst_ref=dst, send_sem=send, recv_sem=recv, device_id=(fi, ti), device_id_type=MESH
        )

    loads = [
        pltpu.make_async_copy(dout, dbuf.at[z, t], lsem.at[0]),
        pltpu.make_async_copy(x_in, xb, lsem.at[1]),
        pltpu.make_async_copy(du_in, ub, lsem.at[2]),
        pltpu.make_async_copy(w, wo, lsem.at[3]),
        pltpu.make_async_copy(y_in, yb, lsem.at[4]),
        pltpu.make_async_copy(z_in, zb, lsem.at[5]),
    ]
    for one in loads:
        one.start()

    barrier = pltpu.get_barrier_semaphore()
    for o in range(1, nf):
        pl.semaphore_signal(barrier, inc=1, device_id=(lax.rem(f + o, nf), t), device_id_type=MESH)
    pl.semaphore_signal(barrier, inc=1, device_id=(f, tx), device_id_type=MESH)
    pl.semaphore_signal(barrier, inc=1, device_id=(f, tc), device_id_type=MESH)
    pl.semaphore_wait(barrier, nf + 1)

    def halo_next():
        return remote(x_in.at[pl.ds(tok - HALO, HALO)], hp, hs.at[0], hr.at[0], f + 1, t)

    def halo_prev(i):
        src = (x_in, du_in)[i]
        return remote(src.at[pl.ds(0, HALO)], hl.at[i], hs.at[1 + i], hr.at[1 + i], f - 1, t)

    @pl.when(f < nf - 1)
    def _():
        halo_next().start()

    @pl.when(f > 0)
    def _():
        halo_prev(0).start()
        halo_prev(1).start()

    def copy_z(zz, sgn):
        return remote(dbuf.at[zz, t], dbuf.at[zz, t], zs.at[zz, (sgn + 1) // 2], dr.at[zz, t], (z + sgn) * 2 + y, t)

    def copy_x(zz):
        return remote(dbuf.at[zz, t], dbuf.at[zz, t], xs.at[zz], dr.at[zz, t], f, tx)

    def copy_c(zz, which):
        tt = (t, tx)[which]
        return remote(dbuf.at[zz, tt], dbuf.at[zz, tt], cs.at[zz, which], dr.at[zz, tt], f, tc)

    def arrived(zz, tt):
        remote(dbuf.at[zz, tt], dbuf.at[zz, tt], cs.at[zz, 0], dr.at[zz, tt], f, tc).wait_recv()

    def copy_w(h):
        return remote(w.at[pl.ds(h * half, half)], wn.at[h], ws.at[h], wr.at[h], yf, t)

    def valid(i):
        return (i >= 0) & (i < nz)

    def around(s, do):
        for sgn in (1, -1):
            zz = z + sgn * s

            @pl.when(valid(zz))
            def _():
                do(zz, sgn)

    loads[0].wait()
    for sgn in (1, -1):

        @pl.when(valid(z + sgn))
        def _():
            copy_z(z, sgn).start()

    copy_x(z).start()
    copy_c(z, 0).start()
    for h in range(2):
        copy_w(h).start()

    @pl.when(f == 0)
    def _():
        hp[...] = jnp.zeros_like(hp)

    @pl.when(f == nf - 1)
    def _():
        hl[...] = jnp.zeros_like(hl)

    loads[1].wait()
    loads[2].wait()

    @pl.when(f > 0)
    def _():
        halo_next().wait_recv()

    @pl.when(f < nf - 1)
    def _():
        halo_prev(0).wait_recv()
        halo_prev(1).wait_recv()

    wide = tb.shape[2]

    def columns(j):
        return pl.ds(pl.multiple_of(j * wide, wide), wide)

    def conv(j, carry):
        cols = columns(j)
        xe[0:8] = hp[:, cols].astype(F32)[8:16]
        xe[8 : 8 + tok] = xb[:, cols].astype(F32)
        xe[8 + tok : 16 + tok] = hl[0, :, cols].astype(F32)[0:8]
        ue[0:tok] = ub[:, cols].astype(F32)
        ue[tok : tok + 8] = hl[1, :, cols].astype(F32)[0:8]
        taps = cw[:, cols]
        pre = cb[:, cols] + jnp.zeros((tok + 8, wide), F32)
        for k in range(KW):
            pre = pre + taps[k : k + 1] * xe[5 + k : 5 + k + tok + 8]
        pe[...] = ue[...] * silu_slope(pre)
        grad_x = jnp.zeros((tok, wide), F32)
        d_pre = pe[0:tok]
        sums = []
        for k in range(KW):
            grad_x = grad_x + taps[k : k + 1] * pe[KW - 1 - k : KW - 1 - k + tok]
            sums.append(jnp.sum(d_pre * xe[5 + k : 5 + k + tok], 0, keepdims=True))
        sums.append(jnp.sum(d_pre, 0, keepdims=True))
        ox[:, cols] = grad_x.astype(BF16)
        tb[j] = jnp.concatenate(sums + [jnp.zeros((3, wide), F32)], 0)
        return carry

    lax.fori_loop(0, nf, conv, 0)

    def tap_out(o):
        to = lax.rem(f + o, nf)
        return remote(tb.at[to], tr.at[f], ts.at[o], trs.at[f], to, t)

    def tap_in(o):
        at = lax.rem(f + o, nf)
        return remote(tb.at[at], tr.at[at], ts.at[o], trs.at[at], at, t)

    def sum_out(o):
        return remote(tg.at[f], tg.at[f], gs.at[o], gr.at[f], lax.rem(f + o, nf), t)

    def sum_in(o):
        at = lax.rem(f + o, nf)
        return remote(tg.at[at], tg.at[at], gs.at[o], gr.at[at], at, t)

    for o in range(1, nf):
        tap_out(o).start()

    part = depth

    def result_own(zz):
        return remote(sbuf.at[zz, pl.ds(0, 2)], rbuf.at[f], ss.at[zz, 0], rr.at[f, 0], zz * 2 + y, t)

    def result_near(zz, h):
        return remote(sbuf.at[zz, 2 + h], rbuf.at[yf, h], ss.at[zz, 1 + h], rr.at[yf, h], zz * 2 + y, t)

    def product(zz, weights, width):
        total = jnp.zeros((tok, width), F32)
        for k in range(nt):
            total = total + lax.dot_general(
                dbuf[zz, k], weights[:, k * part : (k + 1) * part], (((1,), (1,)), ((), ())),
                preferred_element_type=F32,
            )
        return total

    def comp_own(zz):
        total = product(zz, wo, rows)
        sbuf[zz, 0] = total[:, :half]
        sbuf[zz, 1] = total[:, half:]

    def forward(s):
        def do(zz, sgn):
            arrived(zz, t)

            @pl.when(valid(z - sgn))
            def _():
                copy_z(zz, -sgn).start()

            copy_x(zz).start()
            copy_c(zz, 0).start()

        around(s, do)

    def cross(zz, sgn=0):
        arrived(zz, tx)
        copy_c(zz, 1).start()

    def whole(zz):
        arrived(zz, tc)
        arrived(zz, (1 - x) * 2 + 1 - c)

    def own_around(s):
        def step(i, carry):
            zz = z + (1 - 2 * i) * s

            @pl.when(valid(zz))
            def _():
                whole(zz)
                comp_own(zz)
                result_own(zz).start()

            return carry

        lax.fori_loop(0, 2, step, 0)

    forward(1)
    cross(z)
    whole(z)
    loads[3].wait()
    comp_own(z)
    for s in range(2, nz):
        forward(s)
        around(s - 1, cross)
        own_around(s - 1)
        if s == 2:
            total = tb[f]
            for o in range(1, nf):
                tap_in(o).wait_recv()
                total = total + tr[lax.rem(f + o, nf)]
            tg[f] = total
            for o in range(1, nf):
                sum_out(o).start()
    around(nz - 1, cross)
    own_around(nz - 1)

    for h in range(2):
        copy_w(h).wait_recv()

        def near(i, carry):
            zz = z + (1 - 2 * lax.rem(i, 2)) * lax.div(i + 2, 2)

            @pl.when(valid(zz))
            def _():
                sbuf[zz, 2 + h] = product(zz, wn.at[h], half)
                result_near(zz, h).start()

            return carry

        lax.fori_loop(0, 2 * (nz - 1), near, 0)
        sbuf[z, 2 + h] = product(z, wn.at[h], half)

    loads[4].wait()
    loads[5].wait()

    def gate(values, at):
        cols = pl.ds(pl.multiple_of(at, half), half)
        gate_f = zb[:, cols].astype(F32)
        sig = jax.nn.sigmoid(gate_f)
        oy[:, cols] = (values * (gate_f * sig)).astype(BF16)
        slope = sig * (1.0 + gate_f * (1.0 - sig))
        oz[:, cols] = (values * yb[:, cols].astype(F32) * slope).astype(BF16)

    for q in range(2):
        gate(sbuf[z, q], f * rows + q * half)
        gate(sbuf[z, 2 + q], yf * rows + q * half)

    def finish_own(i, carry):
        zz = z + (1 - 2 * lax.rem(i, 2)) * lax.div(i + 2, 2)

        @pl.when(valid(zz))
        def _():
            fi = zz * 2 + y
            remote(sbuf.at[zz, pl.ds(0, 2)], rbuf.at[fi], ss.at[zz, 0], rr.at[fi, 0], fi, t).wait_recv()
            for q in range(2):
                gate(rbuf[fi, q], fi * rows + q * half)

        return carry

    lax.fori_loop(0, 2 * (nz - 1), finish_own, 0)
    for h in range(2):

        def finish_near(i, carry):
            zz = z + (1 - 2 * lax.rem(i, 2)) * lax.div(i + 2, 2)

            @pl.when(valid(zz))
            def _():
                fi = zz * 2 + 1 - y
                remote(sbuf.at[zz, 2 + h], rbuf.at[fi, h], ss.at[zz, 1 + h], rr.at[fi, h], zz * 2 + y, t).wait_recv()
                gate(rbuf[fi, h], fi * rows + h * half)

            return carry

        lax.fori_loop(0, 2 * (nz - 1), finish_near, 0)

    for o in range(1, nf):
        sum_in(o).wait_recv()
    for j in range(nf):
        owb[:, j * wide : (j + 1) * wide] = tg[j]
    for o in range(1, nf):
        tap_out(o).wait_send()
        sum_out(o).wait_send()

    @pl.when(f < nf - 1)
    def _():
        halo_next().wait_send()

    @pl.when(f > 0)
    def _():
        halo_prev(0).wait_send()
        halo_prev(1).wait_send()

    for h in range(2):
        copy_w(h).wait_send()
    for sgn in (1, -1):

        @pl.when(valid(z + sgn))
        def _():
            copy_z(z, sgn).wait_send()

    def sent(zz):
        copy_x(zz).wait_send()
        copy_c(zz, 0).wait_send()
        copy_c(zz, 1).wait_send()

    def drain(zz, sgn):
        @pl.when(valid(z - sgn))
        def _():
            copy_z(zz, -sgn).wait_send()

        sent(zz)
        result_own(zz).wait_send()
        for h in range(2):
            result_near(zz, h).wait_send()

    sent(z)
    for s in range(1, nz):
        around(s, drain)


def fused(nf, nt, dout, w_out, y_scan, z_gate, x_conv, du_scan, conv_w, conv_b):
    tok, depth = dout.shape
    rows = w_out.shape[0]
    width = x_conv.shape[1]
    nz = nf // 2
    wide = width // nf
    anywhere = pl.BlockSpec(memory_space=pl.ANY)
    vmem = pl.BlockSpec(memory_space=pltpu.VMEM)
    dma = pltpu.SemaphoreType.DMA
    grad_y, grad_z, grad_x, sums = pl.pallas_call(
        functools.partial(kernel, nf, nt),
        out_shape=[jax.ShapeDtypeStruct((tok, width), BF16)] * 3 + [jax.ShapeDtypeStruct((8, width), F32)],
        in_specs=[anywhere] * 6 + [vmem] * 2,
        out_specs=[vmem] * 4,
        scratch_shapes=[
            pltpu.VMEM((nz, nt, tok, depth), BF16),
            pltpu.VMEM((rows, nt * depth), BF16),
            pltpu.VMEM((2, rows // 2, nt * depth), BF16),
            pltpu.VMEM((nz, 4, tok, rows // 2), F32),
            pltpu.VMEM((nf, 2, tok, rows // 2), F32),
            pltpu.VMEM((tok, width), BF16),
            pltpu.VMEM((tok, width), BF16),
            pltpu.VMEM((tok, width), BF16),
            pltpu.VMEM((tok, width), BF16),
            pltpu.VMEM((HALO, width), BF16),
            pltpu.VMEM((2, HALO, width), BF16),
            pltpu.VMEM((tok + 16, wide), F32),
            pltpu.VMEM((tok + 8, wide), F32),
            pltpu.VMEM((tok + 8, wide), F32),
            pltpu.VMEM((nf, 8, wide), F32),
            pltpu.VMEM((nf, 8, wide), F32),
            pltpu.VMEM((nf, 8, wide), F32),
            dma((6,)),
            dma((nz, nt)),
            dma((nz, 2)),
            dma((nz,)),
            dma((nz, 2)),
            dma((2,)),
            dma((2,)),
            dma((nz, 3)),
            dma((nf, 2)),
            dma((3,)),
            dma((3,)),
            dma((nf,)),
            dma((nf,)),
            dma((nf,)),
            dma((nf,)),
        ],
        compiler_params=pltpu.CompilerParams(
            collective_id=0, has_side_effects=True, vmem_limit_bytes=48 * 1024 * 1024
        ),
    )(dout, w_out, y_scan, z_gate, x_conv, du_scan, conv_w, conv_b[None, :])
    return grad_y, grad_z, grad_x, sums[:KW], sums[KW]


def shifted(block, axis, distance):
    devices = range(lax.axis_size(axis))
    route = [(i - distance, i) for i in devices if i - distance in devices]
    return lax.ppermute(block, axis, route)


def gathered(dout, w_out, y_scan, z_gate, x_conv, du_scan, conv_w, conv_b):
    tok_rows = x_conv.shape[0]
    width = x_conv.shape[1]
    prior = shifted(x_conv[tok_rows - (KW - 1) :], "fsdp", 1)
    leading = jnp.stack([x_conv[: KW - 1], du_scan[: KW - 1]])
    later = shifted(leading, "fsdp", -1)
    extended = jnp.concatenate([prior, x_conv, later[0]], 0)
    span = tok_rows + KW - 1
    pre_all = jnp.zeros((span, width), F32) + conv_b[None, :]
    for k in range(KW):
        pre_all = pre_all + conv_w[k][None, :] * extended[k : k + span]
    arriving = jnp.concatenate([du_scan, later[1]], 0)
    d_pre_all = arriving.astype(F32) * silu_slope(pre_all)
    d_pre = d_pre_all[:tok_rows]
    grad_x = jnp.zeros((tok_rows, width), F32)
    taps = []
    for k in range(KW):
        grad_x = grad_x + conv_w[k][None, :] * d_pre_all[KW - 1 - k : KW - 1 - k + tok_rows]
        taps.append(jnp.sum(d_pre * extended[k : k + tok_rows], 0))
    grad_w, grad_b = lax.psum((jnp.stack(taps), jnp.sum(d_pre, 0)), "fsdp")
    full_out = lax.all_gather(dout, "tp", axis=1, tiled=True)
    group_w = lax.all_gather(w_out, "fsdp", axis=0, tiled=True)
    d_gated = lax.dot_general(
        full_out, group_w, (((1,), (1,)), ((), ())), preferred_element_type=F32
    )
    gate_f = z_gate.astype(F32)
    grad_y = (d_gated * jax.nn.silu(gate_f)).astype(BF16)
    grad_z = (d_gated * y_scan.astype(F32) * silu_slope(gate_f)).astype(BF16)
    return (grad_y, grad_z, grad_x.astype(BF16), grad_w, grad_b)


def solution(mesh):
    nf, nt = mesh.shape["fsdp"], mesh.shape["tp"]

    def local(dout, w_out, *rest):
        rows = w_out.shape[0]
        kept = nf // 2 * nt * dout.size * 2
        fits = nt == 4 and nf % 2 == 0 and nf >= 6 and rows % 256 == 0 and kept <= 16 * 1024 * 1024
        body = functools.partial(fused, nf, nt) if fits else gathered
        return body(dout, w_out, *rest)

    return jax.shard_map(
        local,
        mesh=mesh,
        in_specs=(
            P("fsdp", "tp"),
            P(("tp", "fsdp"), None),
            P("fsdp", "tp"),
            P("fsdp", "tp"),
            P("fsdp", "tp"),
            P("fsdp", "tp"),
            P(None, "tp"),
            P("tp"),
        ),
        out_specs=(P("fsdp", "tp"), P("fsdp", "tp"), P("fsdp", "tp"), P(None, "tp"), P("tp")),
        check_vma=False,
    )
```

time: 285 us -> 111 us (0.39)
  waiting for transfers between devices: 209 us -> 0 us
  Pallas kernels: 0 us -> 101 us
  blocking collectives: 37.2 us -> 0 us
  between operations: 14.2 us -> 0.66 us
  matrix products: 12.9 us -> 0 us
  local copies, waits for them, and re-layouts: 0.1 us -> 9.07 us
  starting transfers between devices: 6.24 us -> 0 us
  other arithmetic: 5.35 us -> 0 us
    all_gather x2 -> x0, waiting for transfers between devices: 203 us -> none  [the longest x1 203 us: local(): group_w = lax.all_gather(w_out, 'fsdp', axis=0, tiled=True)]
    pallas_call x0 -> x1, Pallas kernels: none -> 101 us  [fused(): pl.pallas_call(functools.partial(kernel, nf, nt), out_shape=[jax.ShapeDty...]
    psum x1 -> x0, blocking collectives: 37.2 us -> none  [local(): grad_w, grad_b = lax.psum((jnp.stack(taps), jnp.sum(d_pre, 0)), 'fsdp')]
    dot_general x1 -> x0, matrix products: 12.9 us -> none  [local(): lax.dot_general(full_out, group_w, (((1,), (1,)), ((), ())), preferred_el...]
    unnamed x12 -> x13, local copies, waits for them, and re-layouts: 0.03 us -> 7.85 us
    ppermute x2 -> x0, starting transfers between devices: 6.16 us -> none  [shifted(): return lax.ppermute(block, axis, route)]
    ppermute x2 -> x0, waiting for transfers between devices: 4.47 us -> none  [shifted(): return lax.ppermute(block, axis, route)]
    reduce_sum x1 -> x0, other arithmetic: 2.99 us -> none  [local(): taps.append(jnp.sum(d_pre * extended[k:k + tok_rows], 0))]
  transfers between devices with their start and end apart: 4 -> 0, of which waited for: 2 -> 0; matrix products, arithmetic and copies ran while one was open for 2% -> 0% of each run, Pallas kernels for 0% -> 0%
where the time goes in v1:
time: 111 us; the launch traced here: 110 us
  Pallas kernels  101 us (91%)
  local copies, waits for them, and re-layouts  9.07 us (8%)
    pallas_call x1, Pallas kernels, fused(): pl.pallas_call(functools.partial(kernel, nf, nt), out_shape=[jax.ShapeDty...  101 us
    unnamed x13, local copies, waits for them, and re-layouts  7.85 us

profile of v1, /device:TPU:0, one launch (start us, length us, event | category | flops | bytes accessed | tf_op | source)
XLA Modules:
  0.0 110.5 jit_solution(7283168633137349114)
XLA Ops:
  0.6 0.0 copy-start
  0.6 1.2 %copy-done = bf16[256,2048]{1,0:T(8,128)(2,1)S(1)} copy-done((bf16[256,2048]{1,0:T(8,128)(2,1)S(1)}, bf16[256,2048]{1,0:T(8,128)(2,1)}, u32[]{:S(2)}) %copy-start) | copy-done | bytes 1048600
  1.9 0.0 copy-start.1
  1.9 1.2 %copy-done.1 = bf16[256,2048]{1,0:T(8,128)(2,1)S(1)} copy-done((bf16[256,2048]{1,0:T(8,128)(2,1)S(1)}, bf16[256,2048]{1,0:T(8,128)(2,1)}, u32[]{:S(2)}) %copy-start.1) | copy-done | bytes 1048600
  3.1 0.0 copy-start.2
  3.1 1.0 copy-done.2
  4.1 0.0 copy-start.3
  4.1 0.8 copy-done.3
  4.9 0.0 copy-start.4
  4.9 0.7 copy-done.4
  5.6 100.7 %shard_map.119 = (bf16[256,2048]{1,0:T(8,128)(2,1)S(1)}, bf16[256,2048]{1,0:T(8,128)(2,1)S(1)}, bf16[256,2048]{1,0:T(8,128)(2,1)S(1)}, f32[8,2048]{1,0:T(8,128)S(1)}) custom-call(bf16[256,1024]{1,0:T(8,128)(2,1)S(1)} %copy-done.2, bf16[256,4096]{1,0:T(8,128)(2,1)} %w.1, bf16[256,2048]{1,0:T(8,128)(2,1)S(1)} %copy-done, bf16[256,2048]{1,0:T(8,128)(2,1)S(1)} %copy-done.1, ...), custom_call_target="tpu_custom_call" | custom-call | tf_op jit(solution)/shard_map/pallas_call | solution.py:376
  106.3 0.6 slice.6
  107.0 0.6 slice.7
  107.6 1.0 copy.16
  108.5 1.0 copy.17
  109.5 1.0 copy.18
Async XLA Ops:
  0.6 1.2 %copy-start = (bf16[256,2048]{1,0:T(8,128)(2,1)S(1)}, bf16[256,2048]{1,0:T(8,128)(2,1)}, u32[]{:S(2)}) copy-start(bf16[256,2048]{1,0:T(8,128)(2,1)} %y_in.1) | copy-start | bytes 3145732
  1.9 1.2 %copy-start.1 = (bf16[256,2048]{1,0:T(8,128)(2,1)S(1)}, bf16[256,2048]{1,0:T(8,128)(2,1)}, u32[]{:S(2)}) copy-start(bf16[256,2048]{1,0:T(8,128)(2,1)} %z_in.1) | copy-start | bytes 3145732
  3.1 1.0 copy-start.2
  4.1 0.8 copy-start.3
  4.9 0.7 copy-start.4

commit v2 on v1

--- a/solution.py
+++ b/solution.py
@@ -36,6 +36,7 @@
     tok, depth = dout.shape
     rows = w.shape[0]
     half = rows // 2
+    few = tok // 2
 
     def remote(src, dst, send, recv, fi, ti):
         return pltpu.make_async_remote_copy(
@@ -43,7 +44,8 @@
         )
 
     loads = [
-        pltpu.make_async_copy(dout, dbuf.at[z, t], lsem.at[0]),
+        pltpu.make_async_copy(dout.at[pl.ds(0, few)], dbuf.at[z, t, 0], lsem.at[0]),
+        pltpu.make_async_copy(dout.at[pl.ds(few, few)], dbuf.at[z, t, 1], lsem.at[6]),
         pltpu.make_async_copy(x_in, xb, lsem.at[1]),
         pltpu.make_async_copy(du_in, ub, lsem.at[2]),
         pltpu.make_async_copy(w, wo, lsem.at[3]),
@@ -76,18 +78,22 @@
         halo_prev(0).start()
         halo_prev(1).start()
 
-    def copy_z(zz, sgn):
-        return remote(dbuf.at[zz, t], dbuf.at[zz, t], zs.at[zz, (sgn + 1) // 2], dr.at[zz, t], (z + sgn) * 2 + y, t)
-
-    def copy_x(zz):
-        return remote(dbuf.at[zz, t], dbuf.at[zz, t], xs.at[zz], dr.at[zz, t], f, tx)
-
-    def copy_c(zz, which):
+    def copy_z(zz, h, sgn):
+        at = dbuf.at[zz, t, h]
+        return remote(at, at, zs.at[zz, h, (sgn + 1) // 2], dr.at[zz, t, h], (z + sgn) * 2 + y, t)
+
+    def copy_x(zz, h):
+        at = dbuf.at[zz, t, h]
+        return remote(at, at, xs.at[zz, h], dr.at[zz, t, h], f, tx)
+
+    def copy_c(zz, h, which):
         tt = (t, tx)[which]
-        return remote(dbuf.at[zz, tt], dbuf.at[zz, tt], cs.at[zz, which], dr.at[zz, tt], f, tc)
-
-    def arrived(zz, tt):
-        remote(dbuf.at[zz, tt], dbuf.at[zz, tt], cs.at[zz, 0], dr.at[zz, tt], f, tc).wait_recv()
+        at = dbuf.at[zz, tt, h]
+        return remote(at, at, cs.at[zz, h, which], dr.at[zz, tt, h], f, tc)
+
+    def arrived(zz, tt, h):
+        at = dbuf.at[zz, tt, h]
+        remote(at, at, cs.at[zz, h, 0], dr.at[zz, tt, h], f, tc).wait_recv()
 
     def copy_w(h):
         return remote(w.at[pl.ds(h * half, half)], wn.at[h], ws.at[h], wr.at[h], yf, t)
@@ -103,15 +109,16 @@
             def _():
                 do(zz, sgn)
 
-    loads[0].wait()
-    for sgn in (1, -1):
-
-        @pl.when(valid(z + sgn))
-        def _():
-            copy_z(z, sgn).start()
-
-    copy_x(z).start()
-    copy_c(z, 0).start()
+    for h in range(2):
+        loads[h].wait()
+        for sgn in (1, -1):
+
+            @pl.when(valid(z + sgn))
+            def _():
+                copy_z(z, h, sgn).start()
+
+        copy_c(z, h, 0).start()
+    copy_x(z, 0).start()
     for h in range(2):
         copy_w(h).start()
 
@@ -123,8 +130,8 @@
     def _():
         hl[...] = jnp.zeros_like(hl)
 
-    loads[1].wait()
     loads[2].wait()
+    loads[3].wait()
 
     @pl.when(f > 0)
     def _():
@@ -163,7 +170,8 @@
         tb[j] = jnp.concatenate(sums + [jnp.zeros((3, wide), F32)], 0)
         return carry
 
-    lax.fori_loop(0, nf, conv, 0)
+    first = nf // 2
+    lax.fori_loop(0, first, conv, 0)
 
     def tap_out(o):
         to = lax.rem(f + o, nf)
@@ -180,144 +188,171 @@
         at = lax.rem(f + o, nf)
         return remote(tg.at[at], tg.at[at], gs.at[o], gr.at[at], at, t)
 
-    for o in range(1, nf):
-        tap_out(o).start()
-
     part = depth
 
-    def result_own(zz):
-        return remote(sbuf.at[zz, pl.ds(0, 2)], rbuf.at[f], ss.at[zz, 0], rr.at[f, 0], zz * 2 + y, t)
-
-    def result_near(zz, h):
-        return remote(sbuf.at[zz, 2 + h], rbuf.at[yf, h], ss.at[zz, 1 + h], rr.at[yf, h], zz * 2 + y, t)
-
-    def product(zz, weights, width):
-        total = jnp.zeros((tok, width), F32)
+    def result_own(zz, h):
+        return remote(sbuf.at[zz, h, pl.ds(0, 2)], rbuf.at[f, h], ss.at[zz, h], rr.at[f, h], zz * 2 + y, t)
+
+    def result_near(zz, q):
+        return remote(sbuf.at[zz, :, 2 + q], rbuf.at[yf, :, q], ss.at[zz, 2 + q], rr.at[yf, q], zz * 2 + y, t)
+
+    def dot(a, b):
+        return lax.dot_general(a, b, (((1,), (1,)), ((), ())), preferred_element_type=F32)
+
+    def comp_own(zz, h):
+        total = jnp.zeros((few, rows), F32)
         for k in range(nt):
-            total = total + lax.dot_general(
-                dbuf[zz, k], weights[:, k * part : (k + 1) * part], (((1,), (1,)), ((), ())),
-                preferred_element_type=F32,
-            )
-        return total
-
-    def comp_own(zz):
-        total = product(zz, wo, rows)
-        sbuf[zz, 0] = total[:, :half]
-        sbuf[zz, 1] = total[:, half:]
-
-    def forward(s):
+            total = total + dot(dbuf[zz, k, h], wo[:, k * part : (k + 1) * part])
+        sbuf[zz, h, 0] = total[:, :half]
+        sbuf[zz, h, 1] = total[:, half:]
+
+    def comp_near(zz, q):
+        total = jnp.zeros((tok, half), F32)
+        for k in range(nt):
+            total = total + dot(dbuf[zz, k].reshape(tok, part), wn[q, :, k * part : (k + 1) * part])
+        sbuf[zz, 0, 2 + q] = total[:few]
+        sbuf[zz, 1, 2 + q] = total[few:]
+
+    def forward(s, h):
         def do(zz, sgn):
-            arrived(zz, t)
+            arrived(zz, t, h)
 
             @pl.when(valid(z - sgn))
             def _():
-                copy_z(zz, -sgn).start()
-
-            copy_x(zz).start()
-            copy_c(zz, 0).start()
+                copy_z(zz, h, -sgn).start()
+
+            copy_x(zz, h).start()
+            copy_c(zz, h, 0).start()
 
         around(s, do)
 
-    def cross(zz, sgn=0):
-        arrived(zz, tx)
-        copy_c(zz, 1).start()
-
-    def whole(zz):
-        arrived(zz, tc)
-        arrived(zz, (1 - x) * 2 + 1 - c)
-
-    def own_around(s):
+    def cross(s, h):
+        def do(zz, sgn):
+            arrived(zz, tx, h)
+            copy_c(zz, h, 1).start()
+
+        around(s, do) if s else do(z, 0)
+
+    def whole(zz, h):
+        arrived(zz, tc, h)
+        arrived(zz, (1 - x) * 2 + 1 - c, h)
+
+    def own_around(s, h):
         def step(i, carry):
             zz = z + (1 - 2 * i) * s
 
             @pl.when(valid(zz))
             def _():
-                whole(zz)
-                comp_own(zz)
-                result_own(zz).start()
+                whole(zz, h)
+                comp_own(zz, h)
+                result_own(zz, h).start()
 
             return carry
 
         lax.fori_loop(0, 2, step, 0)
 
-    forward(1)
-    cross(z)
-    whole(z)
-    loads[3].wait()
-    comp_own(z)
-    for s in range(2, nz):
-        forward(s)
-        around(s - 1, cross)
-        own_around(s - 1)
-        if s == 2:
-            total = tb[f]
-            for o in range(1, nf):
-                tap_in(o).wait_recv()
-                total = total + tr[lax.rem(f + o, nf)]
-            tg[f] = total
-            for o in range(1, nf):
-                sum_out(o).start()
-    around(nz - 1, cross)
-    own_around(nz - 1)
+    def near_around(s, q):
+        def step(i, carry):
+            zz = z + (1 - 2 * i) * s
+
+            @pl.when(valid(zz))
+            def _():
+                comp_near(zz, q)
+                result_near(zz, q).start()
+
+            return carry
+
+        lax.fori_loop(0, 2, step, 0)
+
+    def own_here(h):
+        whole(z, h)
+        comp_own(z, h)
+
+    def share_taps():
+        for o in range(1, nf):
+            tap_out(o).start()
+
+    def total_taps():
+        total = tb[f]
+        for o in range(1, nf):
+            tap_in(o).wait_recv()
+            total = total + tr[lax.rem(f + o, nf)]
+        tg[f] = total
+        for o in range(1, nf):
+            sum_out(o).start()
+
+    stages = [(s, h) for s in range(1, nz) for h in range(2)]
+    last = len(stages)
+    for i in range(last + 2):
+        if i < last:
+            forward(*stages[i])
+        if i == 0:
+            cross(0, 0)
+        elif i <= last:
+            cross(*stages[i - 1])
+        if i == 1:
+            copy_x(z, 1).start()
+            lax.fori_loop(first, nf, conv, 0)
+            share_taps()
+        if i >= 2:
+            if i == 2:
+                loads[4].wait()
+            own_around(*stages[i - 2])
+        if i == 3:
+            cross(0, 1)
+            total_taps()
+        if i == last - 1:
+            copy_w(0).wait_recv()
+            near_around(1, 0)
+        if i == last:
+            near_around(2, 0)
+    own_here(0)
+    own_here(1)
+    for s in range(3, nz):
+        near_around(s, 0)
+    copy_w(1).wait_recv()
+    for s in range(1, nz):
+        near_around(s, 1)
+    for q in range(2):
+        comp_near(z, q)
+
+    loads[5].wait()
+    loads[6].wait()
+
+    def gate(values, h, at):
+        here = pl.ds(h * few, few)
+        cols = pl.ds(pl.multiple_of(at, half), half)
+        gate_f = zb[here, cols].astype(F32)
+        sig = jax.nn.sigmoid(gate_f)
+        oy[here, cols] = (values * (gate_f * sig)).astype(BF16)
+        slope = sig * (1.0 + gate_f * (1.0 - sig))
+        oz[here, cols] = (values * yb[here, cols].astype(F32) * slope).astype(BF16)
 
     for h in range(2):
-        copy_w(h).wait_recv()
-
-        def near(i, carry):
+        for q in range(2):
+            gate(sbuf[z, h, q], h, f * rows + q * half)
+            gate(sbuf[z, h, 2 + q], h, yf * rows + q * half)
+
+    def finish(n, near):
+        def step(i, carry):
             zz = z + (1 - 2 * lax.rem(i, 2)) * lax.div(i + 2, 2)
 
             @pl.when(valid(zz))
             def _():
-                sbuf[zz, 2 + h] = product(zz, wn.at[h], half)
-                result_near(zz, h).start()
+                fi = zz * 2 + (1 - y if near else y)
+                into = rbuf.at[fi, :, n] if near else rbuf.at[fi, n]
+                remote(into, into, ss.at[zz, n], rr.at[fi, n], zz * 2 + y, t).wait_recv()
+                for m in range(2):
+                    h, q = (m, n) if near else (n, m)
+                    gate(rbuf[fi, h, q], h, fi * rows + q * half)
 
             return carry
 
-        lax.fori_loop(0, 2 * (nz - 1), near, 0)
-        sbuf[z, 2 + h] = product(z, wn.at[h], half)
-
-    loads[4].wait()
-    loads[5].wait()
-
-    def gate(values, at):
-        cols = pl.ds(pl.multiple_of(at, half), half)
-        gate_f = zb[:, cols].astype(F32)
-        sig = jax.nn.sigmoid(gate_f)
-        oy[:, cols] = (values * (gate_f * sig)).astype(BF16)
-        slope = sig * (1.0 + gate_f * (1.0 - sig))
-        oz[:, cols] = (values * yb[:, cols].astype(F32) * slope).astype(BF16)
-
-    for q in range(2):
-        gate(sbuf[z, q], f * rows + q * half)
-        gate(sbuf[z, 2 + q], yf * rows + q * half)
-
-    def finish_own(i, carry):
-        zz = z + (1 - 2 * lax.rem(i, 2)) * lax.div(i + 2, 2)
-
-        @pl.when(valid(zz))
-        def _():
-            fi = zz * 2 + y
-            remote(sbuf.at[zz, pl.ds(0, 2)], rbuf.at[fi], ss.at[zz, 0], rr.at[fi, 0], fi, t).wait_recv()
-            for q in range(2):
-                gate(rbuf[fi, q], fi * rows + q * half)
-
-        return carry
-
-    lax.fori_loop(0, 2 * (nz - 1), finish_own, 0)
-    for h in range(2):
-
-        def finish_near(i, carry):
-            zz = z + (1 - 2 * lax.rem(i, 2)) * lax.div(i + 2, 2)
-
-            @pl.when(valid(zz))
-            def _():
-                fi = zz * 2 + 1 - y
-                remote(sbuf.at[zz, 2 + h], rbuf.at[fi, h], ss.at[zz, 1 + h], rr.at[fi, h], zz * 2 + y, t).wait_recv()
-                gate(rbuf[fi, h], fi * rows + h * half)
-
-            return carry
-
-        lax.fori_loop(0, 2 * (nz - 1), finish_near, 0)
+        lax.fori_loop(0, 2 * (nz - 1), step, 0)
+
+    for near in (False, True):
+        for n in range(2):
+            finish(n, near)
 
     for o in range(1, nf):
         sum_in(o).wait_recv()
@@ -338,26 +373,30 @@
 
     for h in range(2):
         copy_w(h).wait_send()
-    for sgn in (1, -1):
-
-        @pl.when(valid(z + sgn))
-        def _():
-            copy_z(z, sgn).wait_send()
+    for h in range(2):
+        for sgn in (1, -1):
+
+            @pl.when(valid(z + sgn))
+            def _():
+                copy_z(z, h, sgn).wait_send()
 
     def sent(zz):
-        copy_x(zz).wait_send()
-        copy_c(zz, 0).wait_send()
-        copy_c(zz, 1).wait_send()
+        for h in range(2):
+            copy_x(zz, h).wait_send()
+            copy_c(zz, h, 0).wait_send()
+            copy_c(zz, h, 1).wait_send()
 
     def drain(zz, sgn):
-        @pl.when(valid(z - sgn))
-        def _():
-            copy_z(zz, -sgn).wait_send()
+        for h in range(2):
+
+            @pl.when(valid(z - sgn))
+            def _():
+                copy_z(zz, h, -sgn).wait_send()
+
+            result_own(zz, h).wait_send()
+            result_near(zz, h).wait_send()
 
         sent(zz)
-        result_own(zz).wait_send()
-        for h in range(2):
-            result_near(zz, h).wait_send()
 
     sent(z)
     for s in range(1, nz):
@@ -379,11 +418,11 @@
         in_specs=[anywhere] * 6 + [vmem] * 2,
         out_specs=[vmem] * 4,
         scratch_shapes=[
-            pltpu.VMEM((nz, nt, tok, depth), BF16),
+            pltpu.VMEM((nz, nt, 2, tok // 2, depth), BF16),
             pltpu.VMEM((rows, nt * depth), BF16),
             pltpu.VMEM((2, rows // 2, nt * depth), BF16),
-            pltpu.VMEM((nz, 4, tok, rows // 2), F32),
-            pltpu.VMEM((nf, 2, tok, rows // 2), F32),
+            pltpu.VMEM((nz, 2, 4, tok // 2, rows // 2), F32),
+            pltpu.VMEM((nf, 2, 2, tok // 2, rows // 2), F32),
             pltpu.VMEM((tok, width), BF16),
             pltpu.VMEM((tok, width), BF16),
             pltpu.VMEM((tok, width), BF16),
@@ -396,14 +435,14 @@
             pltpu.VMEM((nf, 8, wide), F32),
             pltpu.VMEM((nf, 8, wide), F32),
             pltpu.VMEM((nf, 8, wide), F32),
-            dma((6,)),
-            dma((nz, nt)),
+            dma((7,)),
+            dma((nz, nt, 2)),
+            dma((nz, 2, 2)),
             dma((nz, 2)),
-            dma((nz,)),
-            dma((nz, 2)),
+            dma((nz, 2, 2)),
             dma((2,)),
             dma((2,)),
-            dma((nz, 3)),
+            dma((nz, 4)),
             dma((nf, 2)),
             dma((3,)),
             dma((3,)),
@@ -413,7 +452,7 @@
             dma((nf,)),
         ],
         compiler_params=pltpu.CompilerParams(
-            collective_id=0, has_side_effects=True, vmem_limit_bytes=48 * 1024 * 1024
+            collective_id=0, has_side_effects=True, vmem_limit_bytes=60 * 1024 * 1024
         ),
     )(dout, w_out, y_scan, z_gate, x_conv, du_scan, conv_w, conv_b[None, :])
     return grad_y, grad_z, grad_x, sums[:KW], sums[KW]

time: 111 us -> 112 us (level)
  Pallas kernels: 101 us -> 104 us
  local copies, waits for them, and re-layouts: 9.07 us -> 7.33 us
    unnamed x13 -> x7, local copies, waits for them, and re-layouts: 7.85 us -> 4.34 us
    pallas_call x1, Pallas kernels: 101 us -> 104 us  [fused(): pl.pallas_call(functools.partial(kernel, nf, nt), out_shape=[jax.ShapeDty...]
    slice x2, local copies, waits for them, and re-layouts: 1.23 us -> 2.99 us  [fused(): return (grad_y, grad_z, grad_x, sums[:KW], sums[KW])]
where the time goes in v2:
time: 112 us
  Pallas kernels  104 us (93%)
  local copies, waits for them, and re-layouts  7.33 us (7%)
    pallas_call x1, Pallas kernels, fused(): pl.pallas_call(functools.partial(kernel, nf, nt), out_shape=[jax.ShapeDty...  104 us
    unnamed x7, local copies, waits for them, and re-layouts  4.34 us
    slice x2, local copies, waits for them, and re-layouts, fused(): return (grad_y, grad_z, grad_x, sums[:KW], sums[KW])  2.99 us

profile of v2, /device:TPU:0, one launch (start us, length us, event | category | flops | bytes accessed | tf_op | source)
XLA Modules:
  0.0 111.7 jit_solution(1013297395957725387)
XLA Ops:
  0.6 103.7 %shard_map.119 = (bf16[256,2048]{1,0:T(8,128)(2,1)}, bf16[256,2048]{1,0:T(8,128)(2,1)}, bf16[256,2048]{1,0:T(8,128)(2,1)}, f32[8,2048]{1,0:T(8,128)}) custom-call(bf16[256,1024]{1,0:T(8,128)(2,1)} %dout.1, bf16[256,4096]{1,0:T(8,128)(2,1)} %w.1, bf16[256,2048]{1,0:T(8,128)(2,1)} %y_in.1, bf16[256,2048]{1,0:T(8,128)(2,1)} %z_in.1, bf16[256,2048]{1,0:T(8,128)(2,1)} %x_in.1, ...), custom_call_target="tpu_custom_call" | custom-call | tf_op jit(solution)/shard_map/pallas_call | solution.py:415
  104.3 0.0 copy-start.1
  104.3 1.5 %slice.6 = f32[4,2048]{1,0:T(4,128)} slice(f32[8,2048]{1,0:T(8,128)} %get-tuple-element.12), slice={[0:4], [0:2048]} | slice | bytes 65536 | tf_op jit(solution)/shard_map/slice | solution.py:458
  105.9 1.4 %slice.7 = f32[1,2048]{1,0:T(1,128)} slice(f32[8,2048]{1,0:T(8,128)} %get-tuple-element.12), slice={[4:5], [0:2048]} | slice | bytes 16384 | tf_op jit(solution)/shard_map/slice | solution.py:458
  107.3 0.0 copy-start
  107.3 2.4 %copy.16 = bf16[256,2048]{1,0:T(8,128)(2,1)} copy(bf16[256,2048]{1,0:T(8,128)(2,1)} %get-tuple-element.18) | data formatting | bytes 2097152
  109.7 0.0 copy-done.1
  109.7 1.0 copy.17
  110.7 0.0 copy-done
  110.7 1.0 copy.18
Async XLA Ops:
  104.3 5.4 %copy-start.1 = (bf16[256,2048]{1,0:T(8,128)(2,1)S(1)}, bf16[256,2048]{1,0:T(8,128)(2,1)}, u32[]{:S(2)}) copy-start(bf16[256,2048]{1,0:T(8,128)(2,1)} %get-tuple-element.19) | copy-start | bytes 3145732
  107.3 3.4 %copy-start = (bf16[256,2048]{1,0:T(8,128)(2,1)S(1)}, bf16[256,2048]{1,0:T(8,128)(2,1)}, u32[]{:S(2)}) copy-start(bf16[256,2048]{1,0:T(8,128)(2,1)} %get-tuple-element.20) | copy-start | bytes 3145732

commit v3 on v2

--- a/solution.py
+++ b/solution.py
@@ -22,7 +22,7 @@
 def kernel(
     nf, nt, dout, w, y_in, z_in, x_in, du_in, cw, cb,
     oy, oz, ox, owb,
-    dbuf, wo, wn, sbuf, rbuf, xb, ub, yb, zb, hp, hl, xe, ue, pe, tb, tr, tg,
+    dbuf, wo, wn, wot, wnt, sbuf, rbuf, xb, ub, yb, zb, hp, hl, xe, ue, pe, tb, tr, tg,
     lsem, dr, zs, xs, cs, ws, wr, ss, rr, hs, hr, ts, trs, gs, gr,
 ):
     nz = nf // 2
@@ -119,8 +119,7 @@
 
         copy_c(z, h, 0).start()
     copy_x(z, 0).start()
-    for h in range(2):
-        copy_w(h).start()
+    copy_w(0).start()
 
     @pl.when(f == 0)
     def _():
@@ -197,19 +196,23 @@
         return remote(sbuf.at[zz, :, 2 + q], rbuf.at[yf, :, q], ss.at[zz, 2 + q], rr.at[yf, q], zz * 2 + y, t)
 
     def dot(a, b):
-        return lax.dot_general(a, b, (((1,), (1,)), ((), ())), preferred_element_type=F32)
+        return jnp.dot(a, b, preferred_element_type=F32)
+
+    def turn(src, dst):
+        for k in range(nt):
+            dst[k] = src[:, k * part : (k + 1) * part].T
 
     def comp_own(zz, h):
         total = jnp.zeros((few, rows), F32)
         for k in range(nt):
-            total = total + dot(dbuf[zz, k, h], wo[:, k * part : (k + 1) * part])
+            total = total + dot(dbuf[zz, k, h], wot[k])
         sbuf[zz, h, 0] = total[:, :half]
         sbuf[zz, h, 1] = total[:, half:]
 
     def comp_near(zz, q):
         total = jnp.zeros((tok, half), F32)
         for k in range(nt):
-            total = total + dot(dbuf[zz, k].reshape(tok, part), wn[q, :, k * part : (k + 1) * part])
+            total = total + dot(dbuf[zz, k].reshape(tok, part), wnt[k])
         sbuf[zz, 0, 2 + q] = total[:few]
         sbuf[zz, 1, 2 + q] = total[few:]
 
@@ -294,15 +297,19 @@
             copy_x(z, 1).start()
             lax.fori_loop(first, nf, conv, 0)
             share_taps()
+            loads[4].wait()
+            turn(wo, wot)
         if i >= 2:
-            if i == 2:
-                loads[4].wait()
             own_around(*stages[i - 2])
+        if i == 2:
+            copy_w(0).wait_send()
+            copy_w(1).start()
         if i == 3:
             cross(0, 1)
             total_taps()
         if i == last - 1:
             copy_w(0).wait_recv()
+            turn(wn.at[0], wnt)
             near_around(1, 0)
         if i == last:
             near_around(2, 0)
@@ -310,11 +317,12 @@
     own_here(1)
     for s in range(3, nz):
         near_around(s, 0)
+    comp_near(z, 0)
     copy_w(1).wait_recv()
+    turn(wn.at[1], wnt)
     for s in range(1, nz):
         near_around(s, 1)
-    for q in range(2):
-        comp_near(z, q)
+    comp_near(z, 1)
 
     loads[5].wait()
     loads[6].wait()
@@ -371,8 +379,7 @@
         halo_prev(0).wait_send()
         halo_prev(1).wait_send()
 
-    for h in range(2):
-        copy_w(h).wait_send()
+    copy_w(1).wait_send()
     for h in range(2):
         for sgn in (1, -1):
 
@@ -409,7 +416,7 @@
     width = x_conv.shape[1]
     nz = nf // 2
     wide = width // nf
-    anywhere = pl.BlockSpec(memory_space=pl.ANY)
+    anywhere = pl.BlockSpec(memory_space=pltpu.HBM)
     vmem = pl.BlockSpec(memory_space=pltpu.VMEM)
     dma = pltpu.SemaphoreType.DMA
     grad_y, grad_z, grad_x, sums = pl.pallas_call(
@@ -421,6 +428,8 @@
             pltpu.VMEM((nz, nt, 2, tok // 2, depth), BF16),
             pltpu.VMEM((rows, nt * depth), BF16),
             pltpu.VMEM((2, rows // 2, nt * depth), BF16),
+            pltpu.VMEM((nt, depth, rows), BF16),
+            pltpu.VMEM((nt, depth, rows // 2), BF16),
             pltpu.VMEM((nz, 2, 4, tok // 2, rows // 2), F32),
             pltpu.VMEM((nf, 2, 2, tok // 2, rows // 2), F32),
             pltpu.VMEM((tok, width), BF16),
@@ -452,7 +461,7 @@
             dma((nf,)),
         ],
         compiler_params=pltpu.CompilerParams(
-            collective_id=0, has_side_effects=True, vmem_limit_bytes=60 * 1024 * 1024
+            collective_id=0, has_side_effects=True, vmem_limit_bytes=48 * 1024 * 1024
         ),
     )(dout, w_out, y_scan, z_gate, x_conv, du_scan, conv_w, conv_b[None, :])
     return grad_y, grad_z, grad_x, sums[:KW], sums[KW]

time: 112 us -> 104 us (0.929)
  Pallas kernels: 104 us -> 93.7 us
  local copies, waits for them, and re-layouts: 7.33 us -> 9.07 us
    pallas_call x1, Pallas kernels: 104 us -> 93.7 us  [fused(): pl.pallas_call(functools.partial(kernel, nf, nt), out_shape=[jax.ShapeDty...]
    unnamed x7 -> x13, local copies, waits for them, and re-layouts: 4.34 us -> 7.85 us
    slice x2, local copies, waits for them, and re-layouts: 2.99 us -> 1.23 us  [fused(): return (grad_y, grad_z, grad_x, sums[:KW], sums[KW])]
where the time goes in v3:
time: 104 us; the launch traced here: 103 us
  Pallas kernels  93.7 us (90%)
  local copies, waits for them, and re-layouts  9.07 us (9%)
    pallas_call x1, Pallas kernels, fused(): pl.pallas_call(functools.partial(kernel, nf, nt), out_shape=[jax.ShapeDty...  93.7 us
    unnamed x13, local copies, waits for them, and re-layouts  7.85 us

profile of v3, /device:TPU:0, one launch (start us, length us, event | category | flops | bytes accessed | tf_op | source)
XLA Modules:
  0.0 103.5 jit_solution(3346272317373238659)
XLA Ops:
  0.6 0.0 copy-start
  0.6 1.2 %copy-done = bf16[256,2048]{1,0:T(8,128)(2,1)S(1)} copy-done((bf16[256,2048]{1,0:T(8,128)(2,1)S(1)}, bf16[256,2048]{1,0:T(8,128)(2,1)}, u32[]{:S(2)}) %copy-start) | copy-done | bytes 1048600
  1.9 0.0 copy-start.1
  1.9 1.2 %copy-done.1 = bf16[256,2048]{1,0:T(8,128)(2,1)S(1)} copy-done((bf16[256,2048]{1,0:T(8,128)(2,1)S(1)}, bf16[256,2048]{1,0:T(8,128)(2,1)}, u32[]{:S(2)}) %copy-start.1) | copy-done | bytes 1048600
  3.1 0.0 copy-start.2
  3.1 1.0 %copy-done.2 = bf16[256,1024]{1,0:T(8,128)(2,1)S(1)} copy-done((bf16[256,1024]{1,0:T(8,128)(2,1)S(1)}, bf16[256,1024]{1,0:T(8,128)(2,1)}, u32[]{:S(2)}) %copy-start.2) | copy-done | bytes 524312
  4.1 0.0 copy-start.3
  4.1 0.8 copy-done.3
  4.9 0.0 copy-start.4
  4.9 0.7 copy-done.4
  5.6 93.7 %shard_map.119 = (bf16[256,2048]{1,0:T(8,128)(2,1)S(1)}, bf16[256,2048]{1,0:T(8,128)(2,1)S(1)}, bf16[256,2048]{1,0:T(8,128)(2,1)S(1)}, f32[8,2048]{1,0:T(8,128)S(1)}) custom-call(bf16[256,1024]{1,0:T(8,128)(2,1)S(1)} %copy-done.2, bf16[256,4096]{1,0:T(8,128)(2,1)} %w.1, bf16[256,2048]{1,0:T(8,128)(2,1)S(1)} %copy-done, bf16[256,2048]{1,0:T(8,128)(2,1)S(1)} %copy-done.1, ...), custom_call_target="tpu_custom_call" | custom-call | tf_op jit(solution)/shard_map/pallas_call | solution.py:422
  99.3 0.6 slice.6
  99.9 0.6 slice.7
  100.6 1.0 copy.16
  101.5 1.0 copy.17
  102.5 1.0 copy.18
Async XLA Ops:
  0.6 1.2 %copy-start = (bf16[256,2048]{1,0:T(8,128)(2,1)S(1)}, bf16[256,2048]{1,0:T(8,128)(2,1)}, u32[]{:S(2)}) copy-start(bf16[256,2048]{1,0:T(8,128)(2,1)} %y_in.1) | copy-start | bytes 3145732
  1.9 1.2 %copy-start.1 = (bf16[256,2048]{1,0:T(8,128)(2,1)S(1)}, bf16[256,2048]{1,0:T(8,128)(2,1)}, u32[]{:S(2)}) copy-start(bf16[256,2048]{1,0:T(8,128)(2,1)} %z_in.1) | copy-start | bytes 3145732
  3.1 1.0 %copy-start.2 = (bf16[256,1024]{1,0:T(8,128)(2,1)S(1)}, bf16[256,1024]{1,0:T(8,128)(2,1)}, u32[]{:S(2)}) copy-start(bf16[256,1024]{1,0:T(8,128)(2,1)} %dout.1) | copy-start | bytes 1572868
  4.1 0.8 copy-start.3
  4.9 0.7 copy-start.4

commit v4 on v3

--- a/solution.py
+++ b/solution.py
@@ -21,7 +21,7 @@
 
 def kernel(
     nf, nt, dout, w, y_in, z_in, x_in, du_in, cw, cb,
-    oy, oz, ox, owb,
+    oy, oz, ox, ow, ob,
     dbuf, wo, wn, wot, wnt, sbuf, rbuf, xb, ub, yb, zb, hp, hl, xe, ue, pe, tb, tr, tg,
     lsem, dr, zs, xs, cs, ws, wr, ss, rr, hs, hr, ts, trs, gs, gr,
 ):
@@ -120,26 +120,6 @@
         copy_c(z, h, 0).start()
     copy_x(z, 0).start()
     copy_w(0).start()
-
-    @pl.when(f == 0)
-    def _():
-        hp[...] = jnp.zeros_like(hp)
-
-    @pl.when(f == nf - 1)
-    def _():
-        hl[...] = jnp.zeros_like(hl)
-
-    loads[2].wait()
-    loads[3].wait()
-
-    @pl.when(f > 0)
-    def _():
-        halo_next().wait_recv()
-
-    @pl.when(f < nf - 1)
-    def _():
-        halo_prev(0).wait_recv()
-        halo_prev(1).wait_recv()
 
     wide = tb.shape[2]
 
@@ -169,9 +149,6 @@
         tb[j] = jnp.concatenate(sums + [jnp.zeros((3, wide), F32)], 0)
         return carry
 
-    first = nf // 2
-    lax.fori_loop(0, first, conv, 0)
-
     def tap_out(o):
         to = lax.rem(f + o, nf)
         return remote(tb.at[to], tr.at[f], ts.at[o], trs.at[f], to, t)
@@ -283,6 +260,9 @@
         tg[f] = total
         for o in range(1, nf):
             sum_out(o).start()
+
+    loads[4].wait()
+    turn(wo, wot)
 
     stages = [(s, h) for s in range(1, nz) for h in range(2)]
     last = len(stages)
@@ -295,18 +275,12 @@
             cross(*stages[i - 1])
         if i == 1:
             copy_x(z, 1).start()
-            lax.fori_loop(first, nf, conv, 0)
-            share_taps()
-            loads[4].wait()
-            turn(wo, wot)
         if i >= 2:
             own_around(*stages[i - 2])
-        if i == 2:
+        if i == 3:
+            cross(0, 1)
             copy_w(0).wait_send()
             copy_w(1).start()
-        if i == 3:
-            cross(0, 1)
-            total_taps()
         if i == last - 1:
             copy_w(0).wait_recv()
             turn(wn.at[0], wnt)
@@ -324,6 +298,29 @@
         near_around(s, 1)
     comp_near(z, 1)
 
+    @pl.when(f == 0)
+    def _():
+        hp[...] = jnp.zeros_like(hp)
+
+    @pl.when(f == nf - 1)
+    def _():
+        hl[...] = jnp.zeros_like(hl)
+
+    loads[2].wait()
+    loads[3].wait()
+
+    @pl.when(f > 0)
+    def _():
+        halo_next().wait_recv()
+
+    @pl.when(f < nf - 1)
+    def _():
+        halo_prev(0).wait_recv()
+        halo_prev(1).wait_recv()
+
+    lax.fori_loop(0, nf, conv, 0)
+    share_taps()
+
     loads[5].wait()
     loads[6].wait()
 
@@ -358,14 +355,17 @@
 
         lax.fori_loop(0, 2 * (nz - 1), step, 0)
 
-    for near in (False, True):
-        for n in range(2):
-            finish(n, near)
+    for n in range(2):
+        finish(n, False)
+    total_taps()
+    for n in range(2):
+        finish(n, True)
 
     for o in range(1, nf):
         sum_in(o).wait_recv()
     for j in range(nf):
-        owb[:, j * wide : (j + 1) * wide] = tg[j]
+        ow[:, j * wide : (j + 1) * wide] = tg[j, 0:KW]
+        ob[:, j * wide : (j + 1) * wide] = tg[j, KW : KW + 1]
     for o in range(1, nf):
         tap_out(o).wait_send()
         sum_out(o).wait_send()
@@ -419,11 +419,11 @@
     anywhere = pl.BlockSpec(memory_space=pltpu.HBM)
     vmem = pl.BlockSpec(memory_space=pltpu.VMEM)
     dma = pltpu.SemaphoreType.DMA
-    grad_y, grad_z, grad_x, sums = pl.pallas_call(
+    grad_y, grad_z, grad_x, grad_w, grad_b = pl.pallas_call(
         functools.partial(kernel, nf, nt),
-        out_shape=[jax.ShapeDtypeStruct((tok, width), BF16)] * 3 + [jax.ShapeDtypeStruct((8, width), F32)],
+        out_shape=[jax.ShapeDtypeStruct((tok, width), BF16)] * 3 + [jax.ShapeDtypeStruct((KW, width), F32), jax.ShapeDtypeStruct((1, width), F32)],
         in_specs=[anywhere] * 6 + [vmem] * 2,
-        out_specs=[vmem] * 4,
+        out_specs=[vmem] * 5,
         scratch_shapes=[
             pltpu.VMEM((nz, nt, 2, tok // 2, depth), BF16),
             pltpu.VMEM((rows, nt * depth), BF16),
@@ -461,10 +461,10 @@
             dma((nf,)),
         ],
         compiler_params=pltpu.CompilerParams(
-            collective_id=0, has_side_effects=True, vmem_limit_bytes=48 * 1024 * 1024
+            collective_id=0, has_side_effects=True, vmem_limit_bytes=60 * 1024 * 1024
         ),
     )(dout, w_out, y_scan, z_gate, x_conv, du_scan, conv_w, conv_b[None, :])
-    return grad_y, grad_z, grad_x, sums[:KW], sums[KW]
+    return grad_y, grad_z, grad_x, grad_w, grad_b[0]
 
 
 def shifted(block, axis, distance):

time: 104 us -> 110 us (1.058)
  Pallas kernels: 93.7 us -> 104 us
  local copies, waits for them, and re-layouts: 9.07 us -> 5.62 us
    pallas_call x1, Pallas kernels: 93.7 us -> 104 us  [fused(): pl.pallas_call(functools.partial(kernel, nf, nt), out_shape=[jax.ShapeDty...]
    unnamed x13, local copies, waits for them, and re-layouts: 7.85 us -> 5.62 us
    slice x2 -> x0, local copies, waits for them, and re-layouts: 1.23 us -> none  [fused(): return (grad_y, grad_z, grad_x, sums[:KW], sums[KW])]
where the time goes in v4:
time: 110 us
  Pallas kernels  104 us (95%)
  local copies, waits for them, and re-layouts  5.62 us (5%)
    pallas_call x1, Pallas kernels, fused(): pl.pallas_call(functools.partial(kernel, nf, nt), out_shape=[jax.ShapeDty...  104 us
    unnamed x13, local copies, waits for them, and re-layouts  5.62 us

profile of v4, /device:TPU:0, one launch (start us, length us, event | category | flops | bytes accessed | tf_op | source)
XLA Modules:
  0.0 109.8 jit_solution(5526968314993393791)
XLA Ops:
  0.6 103.6 %shard_map.119 = (bf16[256,2048]{1,0:T(8,128)(2,1)}, bf16[256,2048]{1,0:T(8,128)(2,1)}, bf16[256,2048]{1,0:T(8,128)(2,1)}, f32[4,2048]{1,0:T(4,128)}, f32[1,2048]{1,0:T(1,128)}) custom-call(bf16[256,1024]{1,0:T(8,128)(2,1)} %dout.1, bf16[256,4096]{1,0:T(8,128)(2,1)} %w.1, bf16[256,2048]{1,0:T(8,128)(2,1)} %y_in.1, bf16[256,2048]{1,0:T(8,128)(2,1)} %z_in.1, ...), custom_call_target="tpu_custom_call" | custom-call | tf_op jit(solution)/shard_map/pallas_call | solution.py:422
  104.2 0.0 copy-start.1
  104.2 0.0 copy-start
  104.2 2.5 %copy.18 = bf16[256,2048]{1,0:T(8,128)(2,1)} copy(bf16[256,2048]{1,0:T(8,128)(2,1)} %get-tuple-element.20) | data formatting | bytes 2097152
  106.7 0.0 copy-done.1
  106.7 0.0 copy-start.2
  106.7 0.0 copy-start.3
  106.7 1.0 copy.19
  107.7 0.0 copy-done
  107.7 1.0 copy.20
  108.6 0.0 copy-done.2
  108.6 0.6 copy.21
  109.2 0.0 copy-done.3
  109.2 0.6 copy.22
Async XLA Ops:
  104.2 2.5 %copy-start.1 = (bf16[256,2048]{1,0:T(8,128)(2,1)S(1)}, bf16[256,2048]{1,0:T(8,128)(2,1)}, u32[]{:S(2)}) copy-start(bf16[256,2048]{1,0:T(8,128)(2,1)} %get-tuple-element.21) | copy-start | bytes 3145732
  104.2 3.4 %copy-start = (bf16[256,2048]{1,0:T(8,128)(2,1)S(1)}, bf16[256,2048]{1,0:T(8,128)(2,1)}, u32[]{:S(2)}) copy-start(bf16[256,2048]{1,0:T(8,128)(2,1)} %get-tuple-element.22) | copy-start | bytes 3145732
  106.7 1.9 %copy-start.2 = (f32[4,2048]{1,0:T(4,128)S(1)}, f32[4,2048]{1,0:T(4,128)}, u32[]{:S(2)}) copy-start(f32[4,2048]{1,0:T(4,128)} %get-tuple-element.23) | copy-start | bytes 98308
  106.7 2.6 %copy-start.3 = (f32[1,2048]{1,0:T(1,128)S(1)}, f32[1,2048]{1,0:T(1,128)}, u32[]{:S(2)}) copy-start(f32[1,2048]{1,0:T(1,128)} %get-tuple-element.14) | copy-start | bytes 24580

commit v5 on v3

--- a/solution.py
+++ b/solution.py
@@ -21,7 +21,7 @@
 
 def kernel(
     nf, nt, dout, w, y_in, z_in, x_in, du_in, cw, cb,
-    oy, oz, ox, owb,
+    oy, oz, ox, ow, ob,
     dbuf, wo, wn, wot, wnt, sbuf, rbuf, xb, ub, yb, zb, hp, hl, xe, ue, pe, tb, tr, tg,
     lsem, dr, zs, xs, cs, ws, wr, ss, rr, hs, hr, ts, trs, gs, gr,
 ):
@@ -119,27 +119,8 @@
 
         copy_c(z, h, 0).start()
     copy_x(z, 0).start()
-    copy_w(0).start()
-
-    @pl.when(f == 0)
-    def _():
-        hp[...] = jnp.zeros_like(hp)
-
-    @pl.when(f == nf - 1)
-    def _():
-        hl[...] = jnp.zeros_like(hl)
-
-    loads[2].wait()
-    loads[3].wait()
-
-    @pl.when(f > 0)
-    def _():
-        halo_next().wait_recv()
-
-    @pl.when(f < nf - 1)
-    def _():
-        halo_prev(0).wait_recv()
-        halo_prev(1).wait_recv()
+    for h in range(2):
+        copy_w(h).start()
 
     wide = tb.shape[2]
 
@@ -169,9 +150,6 @@
         tb[j] = jnp.concatenate(sums + [jnp.zeros((3, wide), F32)], 0)
         return carry
 
-    first = nf // 2
-    lax.fori_loop(0, first, conv, 0)
-
     def tap_out(o):
         to = lax.rem(f + o, nf)
         return remote(tb.at[to], tr.at[f], ts.at[o], trs.at[f], to, t)
@@ -283,6 +261,29 @@
         tg[f] = total
         for o in range(1, nf):
             sum_out(o).start()
+
+    loads[4].wait()
+    turn(wo, wot)
+
+    @pl.when(f == 0)
+    def _():
+        hp[...] = jnp.zeros_like(hp)
+
+    @pl.when(f == nf - 1)
+    def _():
+        hl[...] = jnp.zeros_like(hl)
+
+    loads[2].wait()
+    loads[3].wait()
+
+    @pl.when(f > 0)
+    def _():
+        halo_next().wait_recv()
+
+    @pl.when(f < nf - 1)
+    def _():
+        halo_prev(0).wait_recv()
+        halo_prev(1).wait_recv()
 
     stages = [(s, h) for s in range(1, nz) for h in range(2)]
     last = len(stages)
@@ -295,24 +296,19 @@
             cross(*stages[i - 1])
         if i == 1:
             copy_x(z, 1).start()
-            lax.fori_loop(first, nf, conv, 0)
-            share_taps()
-            loads[4].wait()
-            turn(wo, wot)
+        conv(i, 0)
         if i >= 2:
             own_around(*stages[i - 2])
-        if i == 2:
-            copy_w(0).wait_send()
-            copy_w(1).start()
         if i == 3:
             cross(0, 1)
-            total_taps()
         if i == last - 1:
             copy_w(0).wait_recv()
             turn(wn.at[0], wnt)
             near_around(1, 0)
         if i == last:
             near_around(2, 0)
+    lax.fori_loop(last + 2, nf, conv, 0)
+    share_taps()
     own_here(0)
     own_here(1)
     for s in range(3, nz):
@@ -323,6 +319,7 @@
     for s in range(1, nz):
         near_around(s, 1)
     comp_near(z, 1)
+    total_taps()
 
     loads[5].wait()
     loads[6].wait()
@@ -358,14 +355,16 @@
 
         lax.fori_loop(0, 2 * (nz - 1), step, 0)
 
-    for near in (False, True):
-        for n in range(2):
-            finish(n, near)
+    for n in range(2):
+        finish(n, False)
+    for n in range(2):
+        finish(n, True)
 
     for o in range(1, nf):
         sum_in(o).wait_recv()
     for j in range(nf):
-        owb[:, j * wide : (j + 1) * wide] = tg[j]
+        ow[:, j * wide : (j + 1) * wide] = tg[j, 0:KW]
+        ob[:, j * wide : (j + 1) * wide] = tg[j, KW : KW + 1]
     for o in range(1, nf):
         tap_out(o).wait_send()
         sum_out(o).wait_send()
@@ -379,7 +378,8 @@
         halo_prev(0).wait_send()
         halo_prev(1).wait_send()
 
-    copy_w(1).wait_send()
+    for h in range(2):
+        copy_w(h).wait_send()
     for h in range(2):
         for sgn in (1, -1):
 
@@ -419,11 +419,11 @@
     anywhere = pl.BlockSpec(memory_space=pltpu.HBM)
     vmem = pl.BlockSpec(memory_space=pltpu.VMEM)
     dma = pltpu.SemaphoreType.DMA
-    grad_y, grad_z, grad_x, sums = pl.pallas_call(
+    grad_y, grad_z, grad_x, grad_w, grad_b = pl.pallas_call(
         functools.partial(kernel, nf, nt),
-        out_shape=[jax.ShapeDtypeStruct((tok, width), BF16)] * 3 + [jax.ShapeDtypeStruct((8, width), F32)],
+        out_shape=[jax.ShapeDtypeStruct((tok, width), BF16)] * 3 + [jax.ShapeDtypeStruct((KW, width), F32), jax.ShapeDtypeStruct((1, width), F32)],
         in_specs=[anywhere] * 6 + [vmem] * 2,
-        out_specs=[vmem] * 4,
+        out_specs=[vmem] * 5,
         scratch_shapes=[
             pltpu.VMEM((nz, nt, 2, tok // 2, depth), BF16),
             pltpu.VMEM((rows, nt * depth), BF16),
@@ -464,7 +464,7 @@
             collective_id=0, has_side_effects=True, vmem_limit_bytes=48 * 1024 * 1024
         ),
     )(dout, w_out, y_scan, z_gate, x_conv, du_scan, conv_w, conv_b[None, :])
-    return grad_y, grad_z, grad_x, sums[:KW], sums[KW]
+    return grad_y, grad_z, grad_x, grad_w, grad_b[0]
 
 
 def shifted(block, axis, distance):
@@ -510,7 +510,7 @@
     def local(dout, w_out, *rest):
         rows = w_out.shape[0]
         kept = nf // 2 * nt * dout.size * 2
-        fits = nt == 4 and nf % 2 == 0 and nf >= 6 and rows % 256 == 0 and kept <= 16 * 1024 * 1024
+        fits = nt == 4 and nf % 2 == 0 and nf >= 8 and rows % 256 == 0 and kept <= 16 * 1024 * 1024
         body = functools.partial(fused, nf, nt) if fits else gathered
         return body(dout, w_out, *rest)
 

time: 104 us -> 107 us (1.029)
  Pallas kernels: 93.7 us -> 97.3 us
    pallas_call x1, Pallas kernels: 93.7 us -> 97.3 us  [fused(): pl.pallas_call(functools.partial(kernel, nf, nt), out_shape=[jax.ShapeDty...]
    slice x2 -> x0, local copies, waits for them, and re-layouts: 1.23 us -> none  [fused(): return (grad_y, grad_z, grad_x, sums[:KW], sums[KW])]
    unnamed x13 -> x15, local copies, waits for them, and re-layouts: 7.85 us -> 9.06 us
where the time goes in v5:
time: 107 us
  Pallas kernels  97.3 us (91%)
  local copies, waits for them, and re-layouts  9.06 us (8%)
    pallas_call x1, Pallas kernels, fused(): pl.pallas_call(functools.partial(kernel, nf, nt), out_shape=[jax.ShapeDty...  97.3 us
    unnamed x15, local copies, waits for them, and re-layouts  9.06 us

profile of v5, /device:TPU:0, one launch (start us, length us, event | category | flops | bytes accessed | tf_op | source)
XLA Modules:
  0.0 107.0 jit_solution(16808602501959708842)
XLA Ops:
  0.6 0.0 copy-start
  0.6 1.2 %copy-done = bf16[256,2048]{1,0:T(8,128)(2,1)S(1)} copy-done((bf16[256,2048]{1,0:T(8,128)(2,1)S(1)}, bf16[256,2048]{1,0:T(8,128)(2,1)}, u32[]{:S(2)}) %copy-start) | copy-done | bytes 1048600
  1.9 0.0 copy-start.1
  1.9 1.2 %copy-done.1 = bf16[256,2048]{1,0:T(8,128)(2,1)S(1)} copy-done((bf16[256,2048]{1,0:T(8,128)(2,1)S(1)}, bf16[256,2048]{1,0:T(8,128)(2,1)}, u32[]{:S(2)}) %copy-start.1) | copy-done | bytes 1048600
  3.1 0.0 copy-start.2
  3.1 1.0 copy-done.2
  4.1 0.0 copy-start.3
  4.1 0.8 copy-done.3
  4.9 0.0 copy-start.4
  4.9 0.7 copy-done.4
  5.6 97.3 %shard_map.119 = (bf16[256,2048]{1,0:T(8,128)(2,1)S(1)}, bf16[256,2048]{1,0:T(8,128)(2,1)S(1)}, bf16[256,2048]{1,0:T(8,128)(2,1)S(1)}, f32[4,2048]{1,0:T(4,128)S(1)}, f32[1,2048]{1,0:T(1,128)S(1)}) custom-call(bf16[256,1024]{1,0:T(8,128)(2,1)S(1)} %copy-done.2, bf16[256,4096]{1,0:T(8,128)(2,1)} %w.1, bf16[256,2048]{1,0:T(8,128)(2,1)S(1)} %copy-done, ...), custom_call_target="tpu_custom_call" | custom-call | tf_op jit(solution)/shard_map/pallas_call | solution.py:422
  102.9 1.0 copy.18
  103.9 1.0 copy.19
  104.9 1.0 copy.20
  105.8 0.6 copy.21
  106.4 0.6 copy.22
Async XLA Ops:
  0.6 1.2 %copy-start = (bf16[256,2048]{1,0:T(8,128)(2,1)S(1)}, bf16[256,2048]{1,0:T(8,128)(2,1)}, u32[]{:S(2)}) copy-start(bf16[256,2048]{1,0:T(8,128)(2,1)} %y_in.1) | copy-start | bytes 3145732
  1.9 1.2 %copy-start.1 = (bf16[256,2048]{1,0:T(8,128)(2,1)S(1)}, bf16[256,2048]{1,0:T(8,128)(2,1)}, u32[]{:S(2)}) copy-start(bf16[256,2048]{1,0:T(8,128)(2,1)} %z_in.1) | copy-start | bytes 3145732
  3.1 1.0 copy-start.2
  4.1 0.8 copy-start.3
  4.9 0.7 copy-start.4

commit v6 on v5

--- a/solution.py
+++ b/solution.py
@@ -95,8 +95,9 @@
         at = dbuf.at[zz, tt, h]
         remote(at, at, cs.at[zz, h, 0], dr.at[zz, tt, h], f, tc).wait_recv()
 
-    def copy_w(h):
-        return remote(w.at[pl.ds(h * half, half)], wn.at[h], ws.at[h], wr.at[h], yf, t)
+    def copy_w(i):
+        src = w.at[pl.ds(i * (half // 2), half // 2)]
+        return remote(src, wn.at[i // 2, pl.ds(i % 2 * (half // 2), half // 2)], ws.at[i], wr.at[i], yf, t)
 
     def valid(i):
         return (i >= 0) & (i < nz)
@@ -119,8 +120,7 @@
 
         copy_c(z, h, 0).start()
     copy_x(z, 0).start()
-    for h in range(2):
-        copy_w(h).start()
+    copy_w(0).start()
 
     wide = tb.shape[2]
 
@@ -296,6 +296,8 @@
             cross(*stages[i - 1])
         if i == 1:
             copy_x(z, 1).start()
+        if i < 3:
+            copy_w(i + 1).start()
         conv(i, 0)
         if i >= 2:
             own_around(*stages[i - 2])
@@ -303,6 +305,7 @@
             cross(0, 1)
         if i == last - 1:
             copy_w(0).wait_recv()
+            copy_w(1).wait_recv()
             turn(wn.at[0], wnt)
             near_around(1, 0)
         if i == last:
@@ -314,13 +317,6 @@
     for s in range(3, nz):
         near_around(s, 0)
     comp_near(z, 0)
-    copy_w(1).wait_recv()
-    turn(wn.at[1], wnt)
-    for s in range(1, nz):
-        near_around(s, 1)
-    comp_near(z, 1)
-    total_taps()
-
     loads[5].wait()
     loads[6].wait()
 
@@ -336,6 +332,16 @@
     for h in range(2):
         for q in range(2):
             gate(sbuf[z, h, q], h, f * rows + q * half)
+    copy_w(2).wait_recv()
+    copy_w(3).wait_recv()
+    turn(wn.at[1], wnt)
+    for s in range(1, nz):
+        near_around(s, 1)
+    comp_near(z, 1)
+    total_taps()
+
+    for h in range(2):
+        for q in range(2):
             gate(sbuf[z, h, 2 + q], h, yf * rows + q * half)
 
     def finish(n, near):
@@ -378,8 +384,8 @@
         halo_prev(0).wait_send()
         halo_prev(1).wait_send()
 
-    for h in range(2):
-        copy_w(h).wait_send()
+    for i in range(4):
+        copy_w(i).wait_send()
     for h in range(2):
         for sgn in (1, -1):
 
@@ -449,8 +455,8 @@
             dma((nz, 2, 2)),
             dma((nz, 2)),
             dma((nz, 2, 2)),
-            dma((2,)),
-            dma((2,)),
+            dma((4,)),
+            dma((4,)),
             dma((nz, 4)),
             dma((nf, 2)),
             dma((3,)),
@@ -461,7 +467,7 @@
             dma((nf,)),
         ],
         compiler_params=pltpu.CompilerParams(
-            collective_id=0, has_side_effects=True, vmem_limit_bytes=48 * 1024 * 1024
+            collective_id=0, has_side_effects=True, vmem_limit_bytes=52 * 1024 * 1024
         ),
     )(dout, w_out, y_scan, z_gate, x_conv, du_scan, conv_w, conv_b[None, :])
     return grad_y, grad_z, grad_x, grad_w, grad_b[0]

time: 107 us -> 107 us (level)
  local copies, waits for them, and re-layouts: 9.06 us -> 7.23 us
  Pallas kernels: 97.3 us -> 98.6 us
    unnamed x15, local copies, waits for them, and re-layouts: 9.06 us -> 7.23 us
    pallas_call x1, Pallas kernels: 97.3 us -> 98.6 us  [fused(): pl.pallas_call(functools.partial(kernel, nf, nt), out_shape=[jax.ShapeDty...]
where the time goes in v6:
time: 107 us; the launch traced here: 106 us
  Pallas kernels  98.6 us (92%)
  local copies, waits for them, and re-layouts  7.23 us (7%)
    pallas_call x1, Pallas kernels, fused(): pl.pallas_call(functools.partial(kernel, nf, nt), out_shape=[jax.ShapeDty...  98.6 us
    unnamed x15, local copies, waits for them, and re-layouts  7.23 us

profile of v6, /device:TPU:0, one launch (start us, length us, event | category | flops | bytes accessed | tf_op | source)
XLA Modules:
  0.0 106.5 jit_solution(13138697180711811069)
XLA Ops:
  0.6 0.0 copy-start
  0.6 1.0 copy-done
  1.7 0.0 copy-start.1
  1.7 0.8 copy-done.1
  2.4 0.0 copy-start.2
  2.4 0.7 copy-done.2
  3.1 98.6 %shard_map.119 = (bf16[256,2048]{1,0:T(8,128)(2,1)S(1)}, bf16[256,2048]{1,0:T(8,128)(2,1)}, bf16[256,2048]{1,0:T(8,128)(2,1)}, f32[4,2048]{1,0:T(4,128)S(1)}, f32[1,2048]{1,0:T(1,128)S(1)}) custom-call(bf16[256,1024]{1,0:T(8,128)(2,1)S(1)} %copy-done, bf16[256,4096]{1,0:T(8,128)(2,1)} %w.1, bf16[256,2048]{1,0:T(8,128)(2,1)} %y_in.1, bf16[256,2048]{1,0:T(8,128)(2,1)} %z_in.1, ...), custom_call_target="tpu_custom_call" | custom-call | tf_op jit(solution)/shard_map/pallas_call | solution.py:428
  101.7 0.0 copy-start.4
  101.7 0.0 copy-start.3
  101.7 1.0 copy.18
  102.7 0.6 copy-done.4
  103.3 1.0 copy.19
  104.3 0.0 copy-done.3
  104.3 1.0 copy.20
  105.3 0.6 copy.21
  105.9 0.6 copy.22
Async XLA Ops:
  0.6 1.0 copy-start
  1.7 0.8 copy-start.1
  2.4 0.7 copy-start.2
  101.7 1.6 %copy-start.4 = (bf16[256,2048]{1,0:T(8,128)(2,1)S(1)}, bf16[256,2048]{1,0:T(8,128)(2,1)}, u32[]{:S(2)}) copy-start(bf16[256,2048]{1,0:T(8,128)(2,1)} %get-tuple-element.21) | copy-start | bytes 3145732
  101.7 2.6 %copy-start.3 = (bf16[256,2048]{1,0:T(8,128)(2,1)S(1)}, bf16[256,2048]{1,0:T(8,128)(2,1)}, u32[]{:S(2)}) copy-start(bf16[256,2048]{1,0:T(8,128)(2,1)} %get-tuple-element.22) | copy-start | bytes 3145732
